TPU v7x, 32 devices: a whole 2x2x4 slice. The times are simulated.
32 devices in a mesh: fit: 2 (over x), pair: 8 (over z, y), blk: 2 (over core).
Axes of the slice: x: 2, y: 2, z: 4, core: 2. Of those that a mesh axis runs over, the one named last changes fastest.
Arguments:
- left_factor: float32 [16, 512, 2048], P('pair', 'blk', 'fit'), may hold values from -2 to 2
- right_factor: float32 [16, 512, 2048], P('pair', None, 'fit'), may hold values from -2 to 2
- amplitudes: float32 [16, 512, 512], P(('pair', 'fit'), 'blk'), may hold values from -6 to 6
- domain_trans: float32 [16, 512, 512], P(('pair', 'fit')), may hold values from -0.25 to 0.25
- vir_energy: float32 [16, 512], P(('pair', 'fit')), may hold values from 0.5 to 3
- occ_energy: float32 [16], P(('pair', 'fit')), may hold values from 0.2 to 1
- coupling: float32 [16, 4], P(('pair', 'fit')), may hold values from -4 to 4
- neighbours: int32 [16, 4], P(('pair', 'fit')), may hold values from 0 to 15, as said below
- dom_blocks: int32 [16], P(('pair', 'fit')), may hold values from 1 to 4
Outputs:
- new_amplitudes: float32 [16, 512, 512], P(('pair', 'fit'), 'blk')
- density_fit: float32 [16, 2048], P('pair', 'fit')
Inputs may be any that keep to these rules, and one draw needn't show every extreme that they name: `neighbours`: with s(p) = p // 2, each entry names a pair p' with (p') % 2 equal to that of the listing pair p, and s(p') equal to s(p), s(p) + 1, s(p) - 1 or s(p) + 4, modulo 8; entries may repeat.
All inputs are finite; a program needn't handle non-finite values.
Results may differ from a plain program's by a relative error of at most 0.000068.
Values sent between devices are 32-bit elements; how exact they have to be, the bound alone decides.
A program may use at most 64 MiB of HBM per device.

v0:
```python
import jax
import jax.numpy as jnp
import numpy as np
from jax import lax
from jax.sharding import PartitionSpec as P


def shifted(block, axis, distance):
    devices = range(lax.axis_size(axis))
    route = [((i - distance) % len(devices), i) for i in devices]
    return lax.ppermute(block, axis, route)


def body(
    left_factor,
    right_factor,
    amplitudes,
    domain_trans,
    vir_energy,
    occ_energy,
    coupling,
    neighbours,
    dom_blocks,
):
    precise = lax.Precision.HIGHEST
    fit_count = lax.axis_size("fit")
    owned = amplitudes.shape[0]
    half_rows = amplitudes.shape[1]
    width = amplitudes.shape[2]
    lefts, rights = (
        lax.all_to_all(left_factor, "fit", split_axis=0, concat_axis=2, tiled=True),
        lax.all_to_all(right_factor, "fit", split_axis=0, concat_axis=2, tiled=True),
    )
    integrals = jnp.einsum("pad,pbd->pab", lefts, rights, precision=precise)
    mixed = jnp.einsum("pab,pcb->pac", amplitudes, domain_trans, precision=precise)
    pair_count = lax.axis_size("pair")
    own_shard = lax.axis_index("pair")
    below = shifted(mixed, "pair", 1)
    above = shifted(mixed, "pair", -1)
    opposite = shifted(mixed, "pair", pair_count // 2)
    candidates = jnp.concatenate([mixed, below, above, opposite], axis=0)
    offsets = np.array([0, pair_count - 1, 1, pair_count // 2], dtype=np.int32)
    slot_offset = jnp.asarray(np.repeat(offsets, owned))
    slot_local = jnp.asarray(np.tile(np.arange(owned, dtype=np.int32), 4))
    shard_of = neighbours // (fit_count * owned)
    local_of = neighbours % owned
    delta = (shard_of - own_shard) % pair_count
    matches = (
        (delta[:, :, None] == slot_offset[None, None, :])
        & (local_of[:, :, None] == slot_local[None, None, :])
    ).astype(jnp.float32)
    weights = jnp.sum(coupling[:, :, None] * matches, axis=1)
    summed = jnp.einsum("pm,mac->pac", weights, candidates, precision=precise)
    correction = jnp.einsum("pac,pcb->pab", summed, domain_trans, precision=precise)
    offset = lax.axis_index("blk") * half_rows
    vir_rows = lax.dynamic_slice_in_dim(vir_energy, offset, half_rows, 1)
    denominator = vir_rows[:, :, None] + vir_energy[:, None, :] + occ_energy[:, None, None]
    residual = integrals + denominator * amplitudes - correction
    limit = dom_blocks * (width // 4)
    row_index = offset + jnp.arange(half_rows, dtype=jnp.int32)
    column_index = jnp.arange(width, dtype=jnp.int32)
    inside = (row_index[None, :, None] < limit[:, None, None]) & (
        column_index[None, None, :] < limit[:, None, None]
    )
    updated = amplitudes - 0.7 * residual / denominator
    new_amplitudes = jnp.where(inside, updated, jnp.zeros_like(updated))
    block_piece = lax.all_gather(new_amplitudes, "fit", axis=0, tiled=True)
    count = block_piece.shape[0]
    left_part = lax.slice_in_dim(left_factor, 0, count, axis=0)
    right_part = lax.slice_in_dim(right_factor, 0, count, axis=0)
    product = jnp.einsum("pab,pbq->paq", block_piece, right_part, precision=precise)
    partial_value = jnp.sum(left_part * product, axis=1)
    density_fit = lax.psum(partial_value, "blk")
    return (new_amplitudes, density_fit)


def solution(mesh):
    placed = (
        P("pair", "blk", "fit"),
        P("pair", None, "fit"),
        P(("pair", "fit"), "blk", None),
        P(("pair", "fit"), None, None),
        P(("pair", "fit"), None),
        P(("pair", "fit")),
        P(("pair", "fit"), None),
        P(("pair", "fit"), None),
        P(("pair", "fit")),
    )
    return jax.shard_map(
        body,
        mesh=mesh,
        in_specs=placed,
        out_specs=(P(("pair", "fit"), "blk", None), P("pair", "fit")),
        check_vma=False,
    )
```

profile of v0, /device:TPU:0, one launch (start us, length us, event | category | flops | bytes accessed | tf_op | source)
XLA Modules:
  0.0 136.3 jit_solution(6848395027405876161)
XLA Ops:
  7.2 0.0 copy-start
  7.2 30.2 %all_to_all.30 = f32[2,256,1024]{2,1,0:T(8,128)S(1)} all-to-all(f32[2,256,1024]{2,1,0:T(8,128)} %param.11), channel_id=1, replica_groups=mesh['fit'=2,'pair'=8,'blk'=2] {'fit'}, dimensions={0} | all-to-all | bytes 4194304 | tf_op jit(solution)/shard_map/all_to_all | solution.py:31
  37.4 5.6 %all-to-all-start.1 = ((f32[2,512,1024]{2,1,0:T(8,128)}), f32[2,512,1024]{2,1,0:T(8,128)}, u32[]{:S(2)}, u32[]{:S(2)}) async-start(f32[2,512,1024]{2,1,0:T(8,128)} %param.12), calls=%async_computation.1 | async-start | bytes 8388608 | tf_op jit(solution)/shard_map/all_to_all | solution.py:32
  43.0 0.0 copy-start.1
  43.0 0.0 copy-start.4
  43.0 0.0 copy-start.2
  43.0 0.0 copy-start.3
  43.0 0.0 all-gather.2.cloned.1.call-start
  43.1 2.9 %convolution_bitcast_fusion.1 = f32[1,256,512]{2,1,0:T(8,128)} fusion(f32[1,512,512]{2,1,0:T(8,128)S(1)} %copy-done, f32[1,256,512]{2,1,0:T(8,128)} %param.13), kind=kOutput, calls=%fused_computation.9 | convolution fusion | flops 805306368 | bytes 2097152 | tf_op jit(solution)/shard_map/pab,pcb->pac/dot_general | solution.py:35
  46.0 2.8 %collective-permute-start.2 = (f32[1,256,512]{2,1,0:T(8,128)}, f32[1,256,512]{2,1,0:T(8,128)}, u32[]{:S(2)}, u32[]{:S(2)}) collective-permute-start(f32[1,256,512]{2,1,0:T(8,128)} %convolution_bitcast_fusion.1), channel_id=1, source_target_pairs={{8,0},{10,2},{12,4},{14,6},{0,8},{2,10},{4,12},{6,14},{9,1},{11,3}... | collective-permute-start | bytes 1572872 | tf_op jit(solution)/shard_map/ppermute | solution.py:11
  48.8 2.3 %collective-permute-start.1 = (f32[1,256,512]{2,1,0:T(8,128)}, f32[1,256,512]{2,1,0:T(8,128)}, u32[]{:S(2)}, u32[]{:S(2)}) collective-permute-start(f32[1,256,512]{2,1,0:T(8,128)} %convolution_bitcast_fusion.1), channel_id=1, source_target_pairs={{2,0},{4,2},{6,4},{8,6},{10,8},{12,10},{14,12},{0,14},{3,1},{5,3},... | collective-permute-start | bytes 1572872 | tf_op jit(solution)/shard_map/ppermute | solution.py:11
  51.1 0.0 collective-permute-start
  52.5 0.1 select_reduce_fusion
  52.6 20.1 %collective-permute-done.2 = f32[1,256,512]{2,1,0:T(8,128)} collective-permute-done((f32[1,256,512]{2,1,0:T(8,128)}, f32[1,256,512]{2,1,0:T(8,128)}, u32[]{:S(2)}, u32[]{:S(2)}) %collective-permute-start.2) | collective-permute-done | bytes 524320 | tf_op jit(solution)/shard_map/ppermute | solution.py:11
  72.7 0.8 collective-permute-done
  73.5 1.7 %pad_maximum_fusion = f32[4,256,512]{2,1,0:T(8,128)S(1)} fusion(f32[1,256,512]{2,1,0:T(8,128)} %collective-permute-done.2, f32[1,256,512]{2,1,0:T(8,128)} %collective-permute-done.1, f32[1,256,512]{2,1,0:T(8,128)} %collective-permute-done, f32[1,256,512]{2,1,0:T(8,128)} %convolution_bitcast_fusion.1), kind=kLoop, calls=%fused_computation.2 | loop fusion | flops 1572864 | bytes 4194304 | tf_op jit(solution)/shard_map/concatenate | solution.py:41
  75.2 4.2 %fusion.3 = f32[1,256,512]{2,0,1:T(1,128)S(1)} fusion(f32[4,256,512]{2,1,0:T(8,128)S(1)} %pad_maximum_fusion, f32[4]{0:T(128)S(1)} %select_reduce_fusion), kind=kOutput, calls=%fused_computation.4 | convolution fusion | flops 6291456 | bytes 2621456 | tf_op jit(solution)/shard_map/pm,mac->pac/dot_general | solution.py:53
  79.5 1.9 %convolution_bitcast_fusion = f32[1,256,512]{2,1,0:T(8,128)} fusion(f32[1,512,512]{2,1,0:T(8,128)S(1)} %copy-done, f32[1,256,512]{2,0,1:T(1,128)S(1)} %fusion.3), kind=kOutput, calls=%fused_computation.8 | convolution fusion | flops 805306368 | bytes 2097152 | tf_op jit(solution)/shard_map/pac,pcb->pab/dot_general | solution.py:54
  81.3 8.8 %all-to-all-done.1 = f32[2,512,1024]{2,1,0:T(8,128)} async-done(((f32[2,512,1024]{2,1,0:T(8,128)}), f32[2,512,1024]{2,1,0:T(8,128)}, u32[]{:S(2)}, u32[]{:S(2)}) %all-to-all-start.1) | async-done | bytes 4194336 | tf_op jit(solution)/shard_map/all_to_all | solution.py:32
  90.1 7.0 %fusion.35 = f32[1,256,512]{2,1,0:T(8,128)} fusion(f32[1,256,512]{2,1,0:T(8,128)} %param.13, f32[1,256,512]{2,1,0:T(8,128)} %convolution_bitcast_fusion, f32[2,512,1024]{2,1,0:T(8,128)} %all-to-all-done.1, f32[2,256,1024]{2,1,0:T(8,128)S(1)} %all_to_all.30, f32[]{:T(128)} %bitcast.84, f32[512]{0:T(512)S(1)} %bitcast.85, f32[256]{0:T(256)S(1)} %bitcast.86, ...), kind=kOutput, calls=%fused_computation.15 | convolution fusion | flops 3222536192 | bytes 7868164 | tf_op jit(solution)/shard_map/pad,pbd->pab/dot_general | solution.py:34
  97.1 0.0 all-gather.2.cloned.1.call-update
  97.2 22.4 %all-gather.2.cloned.1.call-done = f32[2,256,512]{2,1,0:T(8,128)} async-done(((f32[1,256,512]{2,1,0:T(8,128)}), f32[2,256,512]{2,1,0:T(8,128)}) %all-gather.2.cloned.1.call-update) | async-done | bytes 1048592 | tf_op jit(solution)/shard_map/all_gather | solution.py:67
  119.5 6.9 %multiply_reduce_fusion = f32[2,1024]{1,0:T(2,128)S(1)} fusion(f32[2,256,1024]{2,1,0:T(8,128)} %param.11, f32[2,256,512]{2,1,0:T(8,128)} %all-gather.2.cloned.1.call-done, f32[2,512,1024]{2,1,0:T(8,128)} %param.12), kind=kOutput, calls=%fused_computation.6 | convolution fusion | flops 3222272000 | bytes 7348224 | tf_op jit(solution)/shard_map/pab,pbq->paq/dot_general | solution.py:71
  126.4 3.1 %psum.7 = f32[2,1024]{1,0:T(2,128)} all-reduce(f32[2,1024]{1,0:T(2,128)S(1)} %multiply_reduce_fusion), channel_id=1, replica_groups=mesh['fit'=2,'pair'=8,'blk'=2] {'blk'}, use_global_device_ids=true, to_apply=%region_2.3 | all-reduce | flops 2048 | bytes 16384 | tf_op jit(solution)/shard_map/psum | solution.py:73
  (10 shorter events, 0.1 us)
Async XLA Ops:
  7.2 35.9 %copy-start = (f32[1,512,512]{2,1,0:T(8,128)S(1)}, f32[1,512,512]{2,1,0:T(8,128)}, u32[]{:S(2)}) copy-start(f32[1,512,512]{2,1,0:T(8,128)} %param.14) | copy-start | bytes 3145732
  37.4 52.7 %all-to-all-start.1 = ((f32[2,512,1024]{2,1,0:T(8,128)}), f32[2,512,1024]{2,1,0:T(8,128)}, u32[]{:S(2)}, u32[]{:S(2)}) async-start(f32[2,512,1024]{2,1,0:T(8,128)} %param.12), calls=%async_computation.1 | async-start | bytes 8388608 | tf_op jit(solution)/shard_map/all_to_all | solution.py:32
  43.0 9.5 %copy-start.1 = (f32[1,512]{1,0:T(1,128)S(1)}, f32[1,512]{1,0:T(1,128)}, u32[]{:S(2)}) copy-start(f32[1,512]{1,0:T(1,128)} %param.15) | copy-start | bytes 6148
  43.0 9.5 %copy-start.4 = (s32[1,4]{1,0:T(1,128)S(1)}, s32[1,4]{1,0:T(1,128)}, u32[]{:S(2)}) copy-start(s32[1,4]{1,0:T(1,128)} %param.18) | copy-start | bytes 52
  43.0 9.5 %copy-start.2 = (f32[1,4]{1,0:T(1,128)S(1)}, f32[1,4]{1,0:T(1,128)}, u32[]{:S(2)}) copy-start(f32[1,4]{1,0:T(1,128)} %param.17) | copy-start | bytes 52
  43.0 9.5 %copy-start.3 = (s32[4]{0:T(128)S(1)}, s32[4]{0:T(128)}, u32[]{:S(2)}) copy-start(s32[4]{0:T(128)} %constant.63.clone) | copy-start | bytes 52
  43.0 76.5 %all-gather.2.cloned.1.call-start = ((), (), s32[]{:S(2)}) async-start(), calls=%async_computation.2 | async-start | bytes 1572864 | tf_op jit(solution)/shard_map/all_gather | solution.py:67
  46.0 26.7 %collective-permute-start.2 = (f32[1,256,512]{2,1,0:T(8,128)}, f32[1,256,512]{2,1,0:T(8,128)}, u32[]{:S(2)}, u32[]{:S(2)}) collective-permute-start(f32[1,256,512]{2,1,0:T(8,128)} %convolution_bitcast_fusion.1), channel_id=1, source_target_pairs={{8,0},{10,2},{12,4},{14,6},{0,8},{2,10},{4,12},{6,14},{9,1},{11,3}... | collective-permute-start | bytes 1572872 | tf_op jit(solution)/shard_map/ppermute | solution.py:11
  48.8 23.9 %collective-permute-start.1 = (f32[1,256,512]{2,1,0:T(8,128)}, f32[1,256,512]{2,1,0:T(8,128)}, u32[]{:S(2)}, u32[]{:S(2)}) collective-permute-start(f32[1,256,512]{2,1,0:T(8,128)} %convolution_bitcast_fusion.1), channel_id=1, source_target_pairs={{2,0},{4,2},{6,4},{8,6},{10,8},{12,10},{14,12},{0,14},{3,1},{5,3},... | collective-permute-start | bytes 1572872 | tf_op jit(solution)/shard_map/ppermute | solution.py:11
  51.1 22.4 %collective-permute-start = (f32[1,256,512]{2,1,0:T(8,128)}, f32[1,256,512]{2,1,0:T(8,128)}, u32[]{:S(2)}, u32[]{:S(2)}) collective-permute-start(f32[1,256,512]{2,1,0:T(8,128)} %convolution_bitcast_fusion.1), channel_id=1, source_target_pairs={{14,0},{0,2},{2,4},{4,6},{6,8},{8,10},{10,12},{12,14},{15,1},{1,3}... | collective-permute-start | bytes 1572872 | tf_op jit(solution)/shard_map/ppermute | solution.py:11
Sparse Core Ops, SparseCore 0:
  97.3 22.1 all-gather.1
where the time goes:
time: 137 us; the launch traced here: 136 us
  waiting for transfers between devices  52 us (38%)
  blocking collectives  33.3 us (24%)
  matrix products  22.9 us (17%)
  between operations  15.5 us (11%)
  starting transfers between devices  10.8 us (8%)
  other arithmetic  1.81 us (1%)
    all_to_all x1, blocking collectives, body(): lax.all_to_all(left_factor, 'fit', split_axis=0, concat_axis=2, tiled=True)  30.2 us
    all_gather x1, waiting for transfers between devices, body(): block_piece = lax.all_gather(new_amplitudes, 'fit', axis=0, tiled=True)  22.4 us
    ppermute x3, waiting for transfers between devices, shifted(): return lax.ppermute(block, axis, route)  20.9 us
    all_to_all x1, waiting for transfers between devices, body(): lax.all_to_all(right_factor, 'fit', split_axis=0, concat_axis=2, tiled=True)  8.75 us
    dot_general x1, matrix products, body(): integrals = jnp.einsum('pad,pbd->pab', lefts, rights, precision=precise)  7.05 us
    dot_general x1, matrix products, body(): jnp.einsum('pab,pbq->paq', block_piece, right_part, precision=precise)  6.86 us
    all_to_all x1, starting transfers between devices, body(): lax.all_to_all(right_factor, 'fit', split_axis=0, concat_axis=2, tiled=True)  5.6 us
    ppermute x3, starting transfers between devices, shifted(): return lax.ppermute(block, axis, route)  5.14 us
  transfers between devices with their start and end apart: 5, of which 4 were waited for; matrix products, arithmetic and copies ran while one was open for 8% of the time, Pallas kernels for 0%

commit v1 on v0

v1 whole, which is shorter than its diff:
```python
import functools

import jax
import jax.numpy as jnp
from jax import lax
from jax.experimental import pallas as pl
from jax.experimental.pallas import tpu as pltpu
from jax.sharding import PartitionSpec as P

MESH = pl.DeviceIdType.MESH
F32 = jnp.float32
BF16 = jnp.bfloat16
CHUNKS = 4
NN = (((1,), (0,)), ((), ()))
NT = (((1,), (1,)), ((), ()))


def halves(x):
    high = x.astype(BF16)
    low = (x - high.astype(F32)).astype(BF16)
    return high, low


def dot(x, y, dims):
    return lax.dot_general(x, y, dims, preferred_element_type=F32)


def dot3(x, y_high, y_low, dims):
    high, low = halves(x)
    rows = x.shape[0]
    both = dot(jnp.concatenate([high, low], axis=0), y_high, dims)
    return both[:rows] + both[rows:] + dot(high, y_low, dims)


def kernel(
    fits, pairs,
    left_hbm, right_hbm, amp_hbm, trans_hbm, vir_ref, occ_ref, coup_ref, neigh_ref, blocks_ref,
    new_hbm, dens_ref,
    left, right, amp, trans, trans_high, trans_low, right_high, right_low,
    mixed, near, part_out, part_in, own_part, base, gain, new, new_in, dens_own, dens_in,
    load_sem, mix_send, mix_recv, part_send, part_recv, new_send, new_recv, dens_send, dens_recv, out_sem,
):
    me = lax.axis_index("pair")
    fit = lax.axis_index("fit")
    blk = lax.axis_index("blk")
    rows, width = amp.shape
    size = rows // CHUNKS

    loads = [
        pltpu.make_async_copy(amp_hbm.at[0], amp, load_sem.at[0]),
        pltpu.make_async_copy(trans_hbm.at[0], trans, load_sem.at[1]),
    ]
    for j in range(fits):
        t = lax.rem(fit + j + 1, fits)
        loads.append(pltpu.make_async_copy(right_hbm.at[t], right.at[t], load_sem.at[2 + 2 * j]))
        loads.append(pltpu.make_async_copy(left_hbm.at[t], left.at[t], load_sem.at[3 + 2 * j]))
    for load in loads:
        load.start()

    steps = (1, pairs - 1, pairs // 2)
    pair_to = [{"pair": lax.rem(me + d, pairs)} for d in steps]
    fit_to = [{"fit": lax.rem(fit + j, fits)} for j in range(1, fits)]
    blk_to = {"blk": 1 - blk}
    barrier = pltpu.get_barrier_semaphore()
    targets = pair_to + fit_to + [blk_to]
    for target in targets:
        pl.semaphore_signal(barrier, inc=1, device_id=target, device_id_type=MESH)

    loads[0].wait()
    loads[1].wait()
    high, low = halves(trans[...])
    trans_high[...] = high
    trans_low[...] = low

    pl.semaphore_wait(barrier, len(targets))

    sends = []
    mix_copies = []
    for c in range(CHUNKS):
        span = pl.ds(c * size, size)
        mixed[span, :] = dot3(amp[span, :], trans_high[...], trans_low[...], NT)
        group = []
        for k in (2, 0, 1):
            copy = pltpu.make_async_remote_copy(
                src_ref=mixed.at[span],
                dst_ref=near.at[k, span],
                send_sem=mix_send.at[k, c],
                recv_sem=mix_recv.at[k, c],
                device_id=pair_to[k],
                device_id_type=MESH,
            )
            copy.start()
            group.append(copy)
        mix_copies.append(group)
        sends.extend(group)

    part_copies = []
    for j in range(fits):
        t = lax.rem(fit + j + 1, fits)
        loads[2 + 2 * j].wait()
        high, low = halves(right[t])
        right_high[t] = high
        right_low[t] = low
        loads[3 + 2 * j].wait()
        for c in range(CHUNKS):
            span = pl.ds(c * size, size)
            value = dot3(left[t, span, :], right_high[t], right_low[t], NT)
            if j == fits - 1:
                own_part[span, :] = value
                continue
            part_out[j, span, :] = value
            copy = pltpu.make_async_remote_copy(
                src_ref=part_out.at[j, span],
                dst_ref=part_in.at[j, span],
                send_sem=part_send.at[j, c],
                recv_sem=part_recv.at[j, c],
                device_id=fit_to[j],
                device_id_type=MESH,
            )
            copy.start()
            part_copies.append((c, copy))
            sends.append(copy)

    column = lax.broadcasted_iota(jnp.int32, (rows, width), 1)
    row = lax.broadcasted_iota(jnp.int32, (rows, width), 0) + blk * rows
    vir = vir_ref[...]
    vir_rows = jnp.sum(jnp.where(row == column, vir, 0.0), axis=1, keepdims=True)
    limit = blocks_ref[0] * (width // 4)
    scale = 0.7 / (vir_rows + vir + occ_ref[0])
    inside = (row < limit) & (column < limit)
    gain[...] = jnp.where(inside, scale, 0.0)
    base[...] = jnp.where(inside, 0.3 * amp[...] - scale * own_part[...], 0.0)

    weights = []
    for d in (0, pairs - 1, 1, pairs // 2):
        weight = jnp.float32(0.0)
        for k in range(coup_ref.shape[1]):
            shard = neigh_ref[0, k] // fits
            delta = lax.rem(shard - me + pairs, pairs)
            weight = weight + jnp.where(delta == d, coup_ref[0, k], 0.0)
        weights.append(weight)

    def density(f, block, span):
        product = dot3(block, right_high[f], right_low[f], NN)
        return jnp.sum(left[f, span, :] * product, axis=0, keepdims=True)

    new_copies = []
    outs = []
    dens_own[...] = jnp.zeros_like(dens_own)

    def others(c):
        span = pl.ds(c * size, size)
        for j in range(1, fits):
            new_copies[c][j - 1].wait_recv()
            f = lax.rem(fit + fits - j, fits)
            dens_own[f] += density(f, new_in[j - 1, span, :], span)

    for c in range(CHUNKS):
        span = pl.ds(c * size, size)
        for copy in mix_copies[c]:
            copy.wait_recv()
        total = weights[0] * mixed[span, :]
        for k in range(3):
            total = total + weights[k + 1] * near[k, span, :]
        value = dot3(total, trans_high[...], trans_low[...], NN)
        for step, copy in part_copies:
            if step == c:
                copy.wait_recv()
        for j in range(fits - 1):
            value = value - part_in[j, span, :]
        value = base[span, :] + gain[span, :] * value
        new[span, :] = value
        group = []
        for j in range(1, fits):
            copy = pltpu.make_async_remote_copy(
                src_ref=new.at[span],
                dst_ref=new_in.at[j - 1, span],
                send_sem=new_send.at[j - 1, c],
                recv_sem=new_recv.at[j - 1, c],
                device_id=fit_to[j - 1],
                device_id_type=MESH,
            )
            copy.start()
            group.append(copy)
            sends.append(copy)
        new_copies.append(group)
        out = pltpu.make_async_copy(new.at[span], new_hbm.at[0, span], out_sem.at[c])
        out.start()
        outs.append(out)
        dens_own[fit] += density(fit, new[span, :], span)
        if c > 0:
            others(c - 1)
    others(CHUNKS - 1)

    copy = pltpu.make_async_remote_copy(
        src_ref=dens_own, dst_ref=dens_in, send_sem=dens_send, recv_sem=dens_recv,
        device_id=blk_to, device_id_type=MESH,
    )
    copy.start()
    for send in sends:
        send.wait_send()
    for out in outs:
        out.wait()
    copy.wait()
    for f in range(fits):
        dens_ref[f : f + 1, :] = dens_own[f] + dens_in[f]


def body(fits, pairs, left, right, amp, trans, vir, occ, coup, neigh, blocks):
    rows, width = amp.shape[1:]
    aux = left.shape[2]
    hbm = pl.BlockSpec(memory_space=pl.ANY)
    vmem = pl.BlockSpec(memory_space=pltpu.VMEM)
    smem = pl.BlockSpec(memory_space=pltpu.SMEM)
    dma = pltpu.SemaphoreType.DMA
    plane = pltpu.VMEM((rows, width), F32)
    flops = 2 * 3 * 2 * (fits * rows * width * aux + rows * width * width)
    return pl.pallas_call(
        functools.partial(kernel, fits, pairs),
        out_shape=(
            jax.ShapeDtypeStruct(amp.shape, F32),
            jax.ShapeDtypeStruct((fits, aux), F32),
        ),
        in_specs=[hbm] * 4 + [vmem] + [smem] * 4,
        out_specs=(hbm, vmem),
        scratch_shapes=[
            pltpu.VMEM((fits, rows, aux), F32),
            pltpu.VMEM((fits, width, aux), F32),
            plane,
            pltpu.VMEM((width, width), F32),
            pltpu.VMEM((width, width), BF16),
            pltpu.VMEM((width, width), BF16),
            pltpu.VMEM((fits, width, aux), BF16),
            pltpu.VMEM((fits, width, aux), BF16),
            plane,
            pltpu.VMEM((3, rows, width), F32),
            pltpu.VMEM((fits - 1, rows, width), F32),
            pltpu.VMEM((fits - 1, rows, width), F32),
            plane,
            plane,
            plane,
            plane,
            pltpu.VMEM((fits - 1, rows, width), F32),
            pltpu.VMEM((fits, 1, aux), F32),
            pltpu.VMEM((fits, 1, aux), F32),
            dma((2 + 2 * fits,)),
            dma((3, CHUNKS)),
            dma((3, CHUNKS)),
            dma((fits - 1, CHUNKS)),
            dma((fits - 1, CHUNKS)),
            dma((fits - 1, CHUNKS)),
            dma((fits - 1, CHUNKS)),
            dma,
            dma,
            dma((CHUNKS,)),
        ],
        compiler_params=pltpu.CompilerParams(
            collective_id=0, has_side_effects=True, vmem_limit_bytes=48 * 2**20
        ),
        cost_estimate=pl.CostEstimate(flops=flops, bytes_accessed=2**23, transcendentals=0),
    )(left, right, amp, trans, vir, occ, coup, neigh, blocks)


def solution(mesh):
    placed = (
        P("pair", "blk", "fit"),
        P("pair", None, "fit"),
        P(("pair", "fit"), "blk", None),
        P(("pair", "fit"), None, None),
        P(("pair", "fit"), None),
        P(("pair", "fit")),
        P(("pair", "fit"), None),
        P(("pair", "fit"), None),
        P(("pair", "fit")),
    )
    return jax.shard_map(
        functools.partial(body, mesh.shape["fit"], mesh.shape["pair"]),
        mesh=mesh,
        in_specs=placed,
        out_specs=(P(("pair", "fit"), "blk", None), P("pair", "fit")),
        check_vma=False,
    )
```

time: 137 us -> 57.2 us (0.42)
  the two profiles are of different devices: /device:TPU:0 before, /device:TPU:5 now
where the time goes in v1:
time: 57.2 us; the launch traced here: 56.9 us
  Pallas kernels  47.7 us (83%)
  local copies, waits for them, and re-layouts  7.23 us (13%)
  between operations  1.95 us (3%)
    pallas_call x1, Pallas kernels, body(): pl.pallas_call(functools.partial(kernel, fits, pairs), out_shape=(jax.Sha...  47.7 us
    unnamed x14, local copies, waits for them, and re-layouts  7.23 us

profile of v1, /device:TPU:5, one launch (start us, length us, event | category | flops | bytes accessed | tf_op | source)
XLA Modules:
  0.0 56.9 jit_solution(10524247803513788372)
XLA Ops:
  1.9 0.0 copy-start
  1.9 1.6 %copy-done = f32[2,256,1024]{2,1,0:T(8,128)S(1)} copy-done((f32[2,256,1024]{2,1,0:T(8,128)S(1)}, f32[2,256,1024]{2,1,0:T(8,128)}, u32[]{:S(2)}) %copy-start) | copy-done | bytes 2097176
  3.5 0.0 copy-start.1
  3.5 1.2 %copy-done.1 = f32[1,512,512]{2,1,0:T(8,128)S(1)} copy-done((f32[1,512,512]{2,1,0:T(8,128)S(1)}, f32[1,512,512]{2,1,0:T(8,128)}, u32[]{:S(2)}) %copy-start.1) | copy-done | bytes 1048600
  4.7 0.0 copy-start.2
  4.7 1.0 %copy-done.2 = f32[1,256,512]{2,1,0:T(8,128)S(1)} copy-done((f32[1,256,512]{2,1,0:T(8,128)S(1)}, f32[1,256,512]{2,1,0:T(8,128)}, u32[]{:S(2)}) %copy-start.2) | copy-done | bytes 524312
  5.8 0.0 copy-start.3
  5.8 0.7 %copy-done.3 = f32[1,512]{1,0:T(1,128)S(1)} copy-done((f32[1,512]{1,0:T(1,128)S(1)}, f32[1,512]{1,0:T(1,128)}, u32[]{:S(2)}) %copy-start.3) | copy-done | bytes 2072
  6.5 0.0 copy-start.4
  6.5 0.7 %copy-done.4 = f32[1,4]{1,0:T(1,128)S(1)} copy-done((f32[1,4]{1,0:T(1,128)S(1)}, f32[1,4]{1,0:T(1,128)}, u32[]{:S(2)}) %copy-start.4) | copy-done | bytes 40
  7.1 0.0 copy-start.5
  7.1 0.7 %copy-done.5 = s32[1,4]{1,0:T(1,128)S(1)} copy-done((s32[1,4]{1,0:T(1,128)S(1)}, s32[1,4]{1,0:T(1,128)}, u32[]{:S(2)}) %copy-start.5) | copy-done | bytes 40
  7.8 47.7 %shard_map.104 = (f32[1,256,512]{2,1,0:T(8,128)S(1)}, f32[2,1024]{1,0:T(2,128)S(1)}) custom-call(f32[2,256,1024]{2,1,0:T(8,128)S(1)} %copy-done, f32[2,512,1024]{2,1,0:T(8,128)} %right_hbm.1, f32[1,256,512]{2,1,0:T(8,128)S(1)} %copy-done.2, f32[1,512,512]{2,1,0:T(8,128)S(1)} %copy-done.1, f32[1,512]{1,0:T(1,128)S(1)} %copy-done.3, f32[1]{0:T(128)S(6)} %copy.13.occ_ref, ...), custom_call_target="tpu_custom_call" | custom-call | flops 4026531840 | bytes 8388608 | tf_op jit(solution)/shard_map/pallas_call | solution.py:218
  55.5 0.8 %copy.15 = f32[1,256,512]{2,1,0:T(8,128)} copy(f32[1,256,512]{2,1,0:T(8,128)S(1)} %get-tuple-element.4) | data formatting | bytes 1048576
  56.3 0.6 %copy.16 = f32[2,1024]{1,0:T(2,128)} copy(f32[2,1024]{1,0:T(2,128)S(1)} %get-tuple-element.5) | data formatting | bytes 16384
Async XLA Ops:
  1.9 1.6 %copy-start = (f32[2,256,1024]{2,1,0:T(8,128)S(1)}, f32[2,256,1024]{2,1,0:T(8,128)}, u32[]{:S(2)}) copy-start(f32[2,256,1024]{2,1,0:T(8,128)} %left_hbm.1) | copy-start | bytes 6291460
  3.5 1.2 %copy-start.1 = (f32[1,512,512]{2,1,0:T(8,128)S(1)}, f32[1,512,512]{2,1,0:T(8,128)}, u32[]{:S(2)}) copy-start(f32[1,512,512]{2,1,0:T(8,128)} %trans_hbm.1) | copy-start | bytes 3145732
  4.7 1.0 %copy-start.2 = (f32[1,256,512]{2,1,0:T(8,128)S(1)}, f32[1,256,512]{2,1,0:T(8,128)}, u32[]{:S(2)}) copy-start(f32[1,256,512]{2,1,0:T(8,128)} %amp_hbm.1) | copy-start | bytes 1572868
  5.8 0.7 %copy-start.3 = (f32[1,512]{1,0:T(1,128)S(1)}, f32[1,512]{1,0:T(1,128)}, u32[]{:S(2)}) copy-start(f32[1,512]{1,0:T(1,128)} %vir_ref.1) | copy-start | bytes 6148
  6.5 0.7 %copy-start.4 = (f32[1,4]{1,0:T(1,128)S(1)}, f32[1,4]{1,0:T(1,128)}, u32[]{:S(2)}) copy-start(f32[1,4]{1,0:T(1,128)} %coup_ref.1) | copy-start | bytes 52
  7.1 0.7 %copy-start.5 = (s32[1,4]{1,0:T(1,128)S(1)}, s32[1,4]{1,0:T(1,128)}, u32[]{:S(2)}) copy-start(s32[1,4]{1,0:T(1,128)} %neigh_ref.1) | copy-start | bytes 52

commit v2 on v1

v2 whole, which is shorter than its diff:
```python
import functools

import jax
import jax.numpy as jnp
from jax import lax
from jax.experimental import pallas as pl
from jax.experimental.pallas import tpu as pltpu
from jax.sharding import PartitionSpec as P

MESH = pl.DeviceIdType.MESH
F32 = jnp.float32
BF16 = jnp.bfloat16
CHUNKS = 4
PARTS = 2
GROUPS = (2, 1, 1)
WINDOW = 1
AHEAD = 1
OWN = 3
NN = (((1,), (0,)), ((), ()))
NT = (((1,), (1,)), ((), ()))


def halves(x):
    high = x.astype(BF16)
    low = (x - high.astype(F32)).astype(BF16)
    return high, low


def dot(x, y, dims):
    return lax.dot_general(x, y, dims, preferred_element_type=F32)


def dot3(x, y_high, y_low, dims):
    high, low = halves(x)
    rows = x.shape[0]
    both = dot(jnp.concatenate([high, low], axis=0), y_high, dims)
    return both[:rows] + both[rows:] + dot(high, y_low, dims)


def kernel(
    fits, pairs,
    left_hbm, right_hbm, amp_hbm, trans_hbm, vir_hbm, occ_hbm, coup_hbm, neigh_hbm, blocks_hbm,
    new_hbm, dens_ref,
    left, right, amp, trans, vir_ref, occ_ref, coup_ref, neigh_ref, blocks_ref,
    trans_high, trans_low, right_high, right_low,
    held, part_out, part_in, own_part, base, gain, new, new_in, dens_own, dens_in,
    load_sem, mix_send, mix_recv, part_send, part_recv, new_send, new_recv, dens_send, dens_recv, out_sem,
):
    me = lax.axis_index("pair")
    fit = lax.axis_index("fit")
    blk = lax.axis_index("blk")
    rows, width = amp.shape
    size = rows // CHUNKS
    part_size = rows // PARTS

    pieces = [
        (amp_hbm.at[0], amp), (trans_hbm.at[0], trans), (vir_hbm, vir_ref), (occ_hbm, occ_ref),
        (coup_hbm, coup_ref), (neigh_hbm, neigh_ref), (blocks_hbm, blocks_ref),
    ]
    small = len(pieces)
    for j in range(fits):
        t = lax.rem(fit + j + 1, fits)
        pieces += [(right_hbm.at[t], right.at[t]), (left_hbm.at[t], left.at[t])]
    loads = [pltpu.make_async_copy(src, dst, load_sem.at[i]) for i, (src, dst) in enumerate(pieces)]
    for load in loads[:small]:
        load.start()

    half = pairs // 2
    place = lax.rem(me, half)
    group = me - place
    low_end = place == 0
    high_end = place == half - 1
    up = group + lax.rem(place + 1, half)
    down = group + lax.rem(place + half - 1, half)
    pair_to = [{"pair": up}, {"pair": down}, {"pair": lax.rem(me + half, pairs)}]
    at_edge = [high_end, low_end]
    fit_to = [{"fit": lax.rem(fit + j, fits)} for j in range(1, fits)]
    blk_to = {"blk": 1 - blk}
    barrier = pltpu.get_barrier_semaphore()
    targets = pair_to + fit_to + [blk_to]
    for target in targets:
        pl.semaphore_signal(barrier, inc=1, device_id=target, device_id_type=MESH)

    def rows_of(c, count=1):
        return pl.ds(c * size, count * size)

    def mix_copy(k, c, source=OWN):
        span = rows_of(c)
        return pltpu.make_async_remote_copy(
            src_ref=held.at[source, span],
            dst_ref=held.at[k, span],
            send_sem=mix_send.at[k, c],
            recv_sem=mix_recv.at[k, c],
            device_id=pair_to[k],
            device_id_type=MESH,
        )

    def send_own(c):
        mix_copy(2, c).start()
        for k in range(2):

            @pl.when(jnp.logical_not(at_edge[k]))
            def _():
                mix_copy(k, c).start()

    def forward(c):
        mix_copy(2, c).wait_recv()
        for k in range(2):

            @pl.when(at_edge[k])
            def _():
                mix_copy(k, c, 2).start()

    loads[0].wait()
    loads[1].wait()
    for load in loads[small:]:
        load.start()
    high, low = halves(trans[...])
    trans_high[...] = high
    trans_low[...] = low

    for c in range(CHUNKS):
        span = rows_of(c)
        held[OWN, span, :] = dot3(amp[span, :], trans_high[...], trans_low[...], NT)
        if c == 0:
            pl.semaphore_wait(barrier, len(targets))
        if c < WINDOW:
            send_own(c)

    part_copies = []
    for j in range(fits):
        t = lax.rem(fit + j + 1, fits)
        loads[small + 2 * j].wait()
        high, low = halves(right[t])
        right_high[t] = high
        right_low[t] = low
        loads[small + 1 + 2 * j].wait()
        for c in range(PARTS):
            span = pl.ds(c * part_size, part_size)
            value = dot3(left[t, span, :], right_high[t], right_low[t], NT)
            if j == fits - 1:
                own_part[span, :] = value
                continue
            part_out[j, span, :] = value
            copy = pltpu.make_async_remote_copy(
                src_ref=part_out.at[j, span],
                dst_ref=part_in.at[j, span],
                send_sem=part_send.at[j, c],
                recv_sem=part_recv.at[j, c],
                device_id=fit_to[j],
                device_id_type=MESH,
            )
            copy.start()
            part_copies.append((c, copy))

    for load in loads[2:small]:
        load.wait()
    column = lax.broadcasted_iota(jnp.int32, (rows, width), 1)
    row = lax.broadcasted_iota(jnp.int32, (rows, width), 0) + blk * rows
    vir = vir_ref[...]
    vir_rows = jnp.sum(jnp.where(row == column, vir, 0.0), axis=1, keepdims=True)
    limit = blocks_ref[0] * (width // 4)
    scale = 0.7 / (vir_rows + vir + occ_ref[0])
    inside = (row < limit) & (column < limit)
    gain[...] = jnp.where(inside, scale, 0.0)
    base[...] = jnp.where(inside, 0.3 * amp[...] - scale * own_part[...], 0.0)

    weights = []
    for d in (pairs - 1, 1, half, 0):
        weight = jnp.float32(0.0)
        for k in range(coup_ref.shape[1]):
            shard = neigh_ref[0, k] // fits
            delta = lax.rem(shard - me + pairs, pairs)
            weight = weight + jnp.where(delta == d, coup_ref[0, k], 0.0)
        weights.append(weight)

    def density(f, block, span):
        product = dot3(block, right_high[f], right_low[f], NN)
        return jnp.sum(left[f, span, :] * product, axis=0, keepdims=True)

    def new_copy(j, c):
        span = rows_of(c)
        return pltpu.make_async_remote_copy(
            src_ref=new.at[span],
            dst_ref=new_in.at[j - 1, span],
            send_sem=new_send.at[j - 1, c],
            recv_sem=new_recv.at[j - 1, c],
            device_id=fit_to[j - 1],
            device_id_type=MESH,
        )

    def out_copy(c):
        span = rows_of(c)
        return pltpu.make_async_copy(new.at[span], new_hbm.at[0, span], out_sem.at[c])

    def others(first, count):
        span = rows_of(first, count)
        for j in range(1, fits):
            for c in range(first, first + count):
                new_copy(j, c).wait_recv()
            f = lax.rem(fit + fits - j, fits)
            dens_own[f] += density(f, new_in[j - 1, span, :], span)

    dens_own[...] = jnp.zeros_like(dens_own)
    first = 0
    pending = None
    groups = list(GROUPS)
    for step in range(CHUNKS + AHEAD):
        if step < CHUNKS:
            if step + WINDOW < CHUNKS:
                mix_copy(2, step).wait_send()
                send_own(step + WINDOW)
            forward(step)
        c = step - AHEAD
        if c < 0:
            continue
        span = rows_of(c)
        mix_copy(0, c).wait_recv()
        mix_copy(1, c).wait_recv()
        total = weights[0] * held[0, span, :]
        for k in range(1, 4):
            total = total + weights[k] * held[k, span, :]
        value = dot3(total, trans_high[...], trans_low[...], NN)
        for part, copy in part_copies:
            if c % (CHUNKS // PARTS) == 0 and part == c // (CHUNKS // PARTS):
                copy.wait_recv()
        for j in range(fits - 1):
            value = value - part_in[j, span, :]
        new[span, :] = base[span, :] + gain[span, :] * value
        for j in range(1, fits):
            new_copy(j, c).start()
        out_copy(c).start()
        if pending is not None:
            others(*pending)
            pending = None
        if c + 1 == first + groups[0]:
            span = rows_of(first, groups[0])
            dens_own[fit] += density(fit, new[span, :], span)
            pending = (first, groups.pop(0))
            first = c + 1
    others(*pending)

    copy = pltpu.make_async_remote_copy(
        src_ref=dens_own, dst_ref=dens_in, send_sem=dens_send, recv_sem=dens_recv,
        device_id=blk_to, device_id_type=MESH,
    )
    copy.start()
    for c in range(CHUNKS):
        for k in range(2):
            mix_copy(k, c).wait_send()
        if c + WINDOW >= CHUNKS:
            mix_copy(2, c).wait_send()
        for j in range(1, fits):
            new_copy(j, c).wait_send()
        out_copy(c).wait()
    for _, part in part_copies:
        part.wait_send()
    copy.wait()
    for f in range(fits):
        dens_ref[f : f + 1, :] = dens_own[f] + dens_in[f]


def deliver(new_hbm, dens_hbm, new_out, dens_out, new, dens, in_sem, out_sem):
    reads = [
        pltpu.make_async_copy(new_hbm, new, in_sem.at[0]),
        pltpu.make_async_copy(dens_hbm, dens, in_sem.at[1]),
    ]
    writes = [
        pltpu.make_async_copy(new, new_out, out_sem.at[0]),
        pltpu.make_async_copy(dens, dens_out, out_sem.at[1]),
    ]
    for read in reads:
        read.start()
    for read, write in zip(reads, writes):
        read.wait()
        write.start()
    for write in writes:
        write.wait()


def body(fits, pairs, left, right, amp, trans, vir, occ, coup, neigh, blocks):
    rows, width = amp.shape[1:]
    aux = left.shape[2]
    hbm = pl.BlockSpec(memory_space=pltpu.HBM)
    vmem = pl.BlockSpec(memory_space=pltpu.VMEM)
    dma = pltpu.SemaphoreType.DMA
    plane = pltpu.VMEM((rows, width), F32)
    square = pltpu.VMEM((width, width), BF16)
    partner = pltpu.VMEM((fits - 1, rows, width), F32)
    flops = 2 * 3 * 2 * (fits * rows * width * aux + rows * width * width)
    results = pl.pallas_call(
        functools.partial(kernel, fits, pairs),
        out_shape=(
            jax.ShapeDtypeStruct(amp.shape, F32),
            jax.ShapeDtypeStruct((fits, aux), F32),
        ),
        in_specs=[hbm] * 9,
        out_specs=(pl.BlockSpec(memory_space=pl.ANY), vmem),
        scratch_shapes=[
            pltpu.VMEM((fits, rows, aux), F32),
            pltpu.VMEM((fits, width, aux), F32),
            plane,
            pltpu.VMEM((width, width), F32),
            pltpu.VMEM(vir.shape, F32),
            pltpu.SMEM(occ.shape, F32),
            pltpu.SMEM(coup.shape, F32),
            pltpu.SMEM(neigh.shape, jnp.int32),
            pltpu.SMEM(blocks.shape, jnp.int32),
            square,
            square,
            pltpu.VMEM((fits, width, aux), BF16),
            pltpu.VMEM((fits, width, aux), BF16),
            pltpu.VMEM((4, rows, width), F32),
            partner,
            partner,
            plane,
            plane,
            plane,
            plane,
            partner,
            pltpu.VMEM((fits, 1, aux), F32),
            pltpu.VMEM((fits, 1, aux), F32),
            dma((7 + 2 * fits,)),
            dma((3, CHUNKS)),
            dma((3, CHUNKS)),
            dma((fits - 1, PARTS)),
            dma((fits - 1, PARTS)),
            dma((fits - 1, CHUNKS)),
            dma((fits - 1, CHUNKS)),
            dma,
            dma,
            dma((CHUNKS,)),
        ],
        compiler_params=pltpu.CompilerParams(
            collective_id=0, has_side_effects=True, vmem_limit_bytes=64 * 2**20
        ),
        cost_estimate=pl.CostEstimate(flops=flops, bytes_accessed=2**23, transcendentals=0),
    )(left, right, amp, trans, vir, occ, coup, neigh, blocks)
    return pl.pallas_call(
        deliver,
        out_shape=tuple(jax.ShapeDtypeStruct(r.shape, F32) for r in results),
        in_specs=[hbm] * 2,
        out_specs=(hbm, hbm),
        scratch_shapes=[pltpu.VMEM(r.shape, F32) for r in results] + [dma((2,)), dma((2,))],
        cost_estimate=pl.CostEstimate(flops=0, bytes_accessed=2**20, transcendentals=0),
    )(*results)


def solution(mesh):
    placed = (
        P("pair", "blk", "fit"),
        P("pair", None, "fit"),
        P(("pair", "fit"), "blk", None),
        P(("pair", "fit"), None, None),
        P(("pair", "fit"), None),
        P(("pair", "fit")),
        P(("pair", "fit"), None),
        P(("pair", "fit"), None),
        P(("pair", "fit")),
    )
    return jax.shard_map(
        functools.partial(body, mesh.shape["fit"], mesh.shape["pair"]),
        mesh=mesh,
        in_specs=placed,
        out_specs=(P(("pair", "fit"), "blk", None), P("pair", "fit")),
        check_vma=False,
    )
```

time: 57.2 us -> 44.7 us (0.78)
  the two profiles are of different devices: /device:TPU:5 before, /device:TPU:0 now
where the time goes in v2:
time: 44.7 us; the launch traced here: 44.5 us
  Pallas kernels  42.6 us (95%)
  between operations  1.93 us (4%)
    pallas_call x1, Pallas kernels, body(): pl.pallas_call(functools.partial(kernel, fits, pairs), out_shape=(jax.Sha...  40.7 us
    pallas_call x1, Pallas kernels, body(): pl.pallas_call(deliver, out_shape=tuple((jax.ShapeDtypeStruct(r.shape, F3...  1.87 us

profile of v2, /device:TPU:0, one launch (start us, length us, event | category | flops | bytes accessed | tf_op | source)
XLA Modules:
  0.0 44.5 jit_solution(5073674199525018429)
XLA Ops:
  1.9 40.7 %shard_map.104 = (f32[1,256,512]{2,1,0:T(8,128)}, f32[2,1024]{1,0:T(2,128)}) custom-call(f32[2,256,1024]{2,1,0:T(8,128)} %left_hbm.1, f32[2,512,1024]{2,1,0:T(8,128)} %right_hbm.1, f32[1,256,512]{2,1,0:T(8,128)} %amp_hbm.1, f32[1,512,512]{2,1,0:T(8,128)} %trans_hbm.1, f32[1,512]{1,0:T(1,128)} %vir_hbm.1, f32[1]{0:T(128)S(6)} %copy.11.occ_hbm, ...), custom_call_target="tpu_custom_call" | custom-call | flops 4026531840 | bytes 8388608 | tf_op jit(solution)/shard_map/pallas_call | solution.py:291
  42.6 1.9 %shard_map.105 = (f32[1,256,512]{2,1,0:T(8,128)}, f32[2,1024]{1,0:T(2,128)}) custom-call(f32[1,256,512]{2,1,0:T(8,128)} %get-tuple-element.4.new_hbm, f32[2,1024]{1,0:T(2,128)} %get-tuple-element.5.dens_hbm), custom_call_target="tpu_custom_call" | custom-call | bytes 1048576 | tf_op jit(solution)/shard_map/pallas_call | solution.py:339
